TPU v7x, 128 devices: a whole 4x4x4 slice. The times are simulated.
128 devices in a mesh: gz: 16 (over x, z_hi, core), gy: 8 (over z_lo, y).
Axes of the slice: x: 4, y: 4, z: 4 (z_hi: 2, z_lo: 2; z = z_hi * 2 + z_lo), core: 2. Of those that a mesh axis runs over, the one named last changes fastest.
Arguments:
- noisy: float32 [64, 512, 512], P('gz', 'gy'), may hold values from -6 to 6
- noise: float32 [64, 512, 512], P(None, 'gy', 'gz'), may hold values from -6 to 6
- timestep: int32 [1], replicated, may hold values from 100 to 599
- measured: float32 [4, 2, 512, 512], P(None, None, 'gz', 'gy'), may hold values from -6 to 6
- cap_index: int32 [4, 512, 512], P(None, 'gz', 'gy'), may hold values from 0 to 63, as said below
- w_patch: bfloat16 [2, 256, 384], replicated, may hold values from -0.375 to 0.375
- w_qkv: bfloat16 [2, 384, 1152], replicated, may hold values from -40 to 40
- w_out: bfloat16 [2, 384, 384], replicated, may hold values from -0.3125 to 0.3125
- w_up: bfloat16 [2, 384, 1536], replicated, may hold values from -0.3125 to 0.3125
- w_down: bfloat16 [2, 1536, 384], replicated, may hold values from -0.15625 to 0.15625
- w_unpatch: bfloat16 [2, 384, 256], replicated, may hold values from -0.3125 to 0.3125
- norm_gain: float32 [2, 3, 384], replicated, may hold values from 0.25 to 1.75
Outputs:
- previous: float32 [64, 512, 512], P(None, 'gy', 'gz')
- estimate: float32 [64, 512, 512], P(None, 'gy', 'gz')
Inputs may be any that keep to these rules, and one draw needn't show every extreme that they name: cap_index[a, ky, kx] is the depth frequency that illumination a measures at lateral frequencies ky, kx; different illuminations may name the same cell.
All inputs are finite; a program needn't handle non-finite values.
Results may differ from a plain program's by a relative error of at most 0.011.
Values may be sent and summed in bfloat16 or wider, within the bound.
A program may use at most 128 MiB of HBM per device.

v0:
```python
import math

import jax
import jax.numpy as jnp
import numpy as np
from jax import lax
from jax.experimental import pallas as pl
from jax.experimental.pallas import tpu as pltpu
from jax.sharding import PartitionSpec as P

PATCH = 16
D = 384
HEADS = 6
FF = 1536
TRAIN_STEPS = 1000
STRIDE = 100
NZ = 64
LAT = 512
GZ = 16
GY = 8
NY = 4
GROUP = GZ * NY
SIDE = LAT // PATCH
HALF = SIDE * SIDE // 2
PIX = PATCH * PATCH
norm_eps = 1e-05
MIB = 1024 * 1024
f32 = jnp.float32
bf16 = jnp.bfloat16
MESH_ID = pl.DeviceIdType.MESH
NT = (((1,), (1,)), ((), ()))
TN = (((0,), (0,)), ((), ()))


def tables():
    parity, half_x, block_y = np.meshgrid(np.arange(2), np.arange(16), np.arange(32), indexing="ij")
    block_x = (2 * half_x + parity).reshape(-1)
    block_y = block_y.reshape(-1)
    by, bx = np.meshgrid(np.arange(32), np.arange(32), indexing="ij")
    by, bx = by.reshape(-1), bx.reshape(-1)
    turn = 2 * np.pi * ((block_y[:, None] * by[None] + block_x[:, None] * bx[None]) % 32) / 32
    coarse = np.concatenate([np.cos(turn), -np.sin(turn)], axis=1)
    xi, yi = np.meshgrid(np.arange(16), np.arange(16), indexing="ij")
    xi, yi = xi.reshape(-1), yi.reshape(-1)
    turn = 2 * np.pi * ((yi[:, None] * by[None] + xi[:, None] * bx[None]) % 512) / 512
    twist = np.stack([np.cos(turn), -np.sin(turn)]) / 32.0
    fine = np.zeros((2, 16, 4, 2, 2, 2, 256))
    for half in range(2):
        for quarter in range(4):
            for rest in range(2):
                ax = 8 * half + 2 * quarter + rest
                turn = 2 * np.pi * ((np.arange(16)[:, None] * yi[None] + ax * xi[None]) % 16) / 16
                fine[half, :, quarter, 0, rest, 0] = np.cos(turn)
                fine[half, :, quarter, 0, rest, 1] = np.sin(turn)
                fine[half, :, quarter, 1, rest, 0] = -np.sin(turn)
                fine[half, :, quarter, 1, rest, 1] = np.cos(turn)
    fine = fine.reshape(2, 256, 512) / 16.0
    to_bf = lambda a: a.astype(jnp.bfloat16)
    order = np.zeros((512, 512), np.float32)
    for gy in range(8):
        for hx in range(16):
            for yb in range(4):
                order[hx * 32 + gy * 4 + yb, gy * 64 + hx * 4 + yb] = 1.0
    swap = np.zeros((256, 256), np.float32)
    for y in range(16):
        for x in range(16):
            swap[x * 16 + y, y * 16 + x] = 1.0
    cast = np.zeros((512, 512), np.float32)
    for xb in range(32):
        for s in range(4):
            for yb in range(4):
                cast[(xb % 2) * 256 + s * 64 + (xb // 2) * 4 + yb, xb * 16 + s * 4 + yb] = 1.0
    deal = np.zeros((512, 512), np.float32)
    for zb in range(4):
        for x in range(4):
            for yb in range(32):
                row = (yb // 4) * 64 + zb * 16 + (yb % 4) * 4 + x
                deal[row, zb * 128 + x * 32 + yb] = 1.0
    return (
        to_bf(coarse),
        twist.astype(np.float32),
        to_bf(fine),
        to_bf(np.ascontiguousarray(fine.transpose(0, 2, 1))),
        to_bf(order),
        to_bf(swap),
        to_bf(cast),
        to_bf(deal),
    )


def cumulative_alpha(moment):
    phase_angle = (moment / TRAIN_STEPS + 0.008) / 1.008 * (math.pi / 2.0)
    return jnp.cos(phase_angle) ** 2


def time_features(moment):
    half_width = D // 2
    frequency = jnp.exp(
        -math.log(10000.0) * jnp.arange(half_width).astype(jnp.float32) / half_width
    )
    angles = moment * frequency
    return jnp.concatenate([jnp.sin(angles), jnp.cos(angles)])


def dot(a, b, dims=None):
    if dims is None:
        return jnp.dot(a, b, preferred_element_type=f32)
    return lax.dot_general(a, b, dims, preferred_element_type=f32)


def norm(values, gain_row):
    average = jnp.mean(values, axis=-1, keepdims=True)
    centred = values - average
    variance = jnp.mean(centred * centred, axis=-1, keepdims=True)
    return (centred * lax.rsqrt(variance + norm_eps) * gain_row).astype(bf16)


def gelu(v):
    return 0.5 * v * (1.0 + jnp.tanh(math.sqrt(2.0 / math.pi) * (v + 0.044715 * (v * v * v))))


def exchange_blocks(arrays, width):
    arrays = list(arrays)
    lane = lax.broadcasted_iota(jnp.int32, arrays[0].shape, 1) // width
    step = 1
    while step < len(arrays):
        low = (lane // step) % 2 == 0
        for i in range(len(arrays)):
            if i & step == 0:
                a, b = arrays[i], arrays[i | step]
                arrays[i] = jnp.where(low, a, pltpu.roll(b, step * width, axis=1))
                arrays[i | step] = jnp.where(low, pltpu.roll(a, 128 - step * width, axis=1), b)
        step *= 2
    return arrays


def attention(queries, keys, values, left):
    outs = []
    for pair in range(HEADS // 2):
        lanes = slice(128 * pair, 128 * pair + 128)
        q, k, v = queries[:, lanes], keys[:, lanes], values[:, lanes]
        halves = []
        for which in range(2):
            q_one = jnp.where(left if which == 0 else ~left, q, jnp.zeros_like(q))
            scores = dot(q_one, k, NT)
            top = jnp.max(scores, axis=-1, keepdims=True)
            raised = jnp.exp(scores - top)
            total = jnp.sum(raised, axis=-1, keepdims=True)
            halves.append(dot(raised.astype(bf16), v) / total)
        outs.append(jnp.where(left, halves[0], halves[1]).astype(bf16))
    return jnp.concatenate(outs, axis=1)


def tail(hidden, attended, w_out, w_up, w_down, gains):
    hidden = hidden + dot(attended, w_out[...])
    normed = norm(hidden, gains[1:2, :])
    inner = gelu(dot(normed, w_up[...])).astype(bf16)
    hidden = hidden + dot(inner, w_down[...])
    return norm(hidden, gains[2:3, :])


CHUNK = 128
PARTS = HALF // CHUNK


def step_kernel(*refs):
    (
        scal, feat, gains, noisy, measured, cap,
        h_patch, h_qkv, h_out, h_up, h_down, h_unpatch,
        h_coarse, h_twist, h_fine, h_fine_t, h_order, h_swap, h_cast, h_deal,
        final_dst, relay_dst,
        patch0, qkv0, out0, up0, down0, unpatch0,
        patch1, qkv1, out1, up1, down1, unpatch1,
        coarse, twist, fine, fine_t, order, swap, cast, deal,
        strips, wide, cut, own_src, own_dst, oth_dst, relay_src,
        tok, low, hidden, queries, pairs, guess, guess16, guess_dst,
        summed, turned, spread, line_src, line_dst,
        cells, fix_src, fix_dst, turned2, spread2, back_src, back_dst, blended,
        col_src, col_dst, rest_src, rest_dst, last, final_src,
        load_sem, send_sem, recv_sem, pair_send, pair_recv,
    ) = refs
    gz, gy = lax.axis_index("gz"), lax.axis_index("gy")
    plane, y = gy // NY, gy % NY
    me = gz * NY + y

    plan = [
        (h_cast, cast), (h_swap, swap), (h_order, order), (h_patch.at[0], patch0),
        (h_qkv.at[0], qkv0), (h_out.at[0], out0), (h_up.at[0], up0), (h_down.at[0], down0),
        (h_unpatch.at[0], unpatch0), (h_coarse, coarse), (h_twist, twist),
        (h_fine.at[plane], fine), (h_fine_t.at[plane], fine_t),
        (h_patch.at[1], patch1), (h_qkv.at[1], qkv1), (h_out.at[1], out1), (h_up.at[1], up1),
        (h_down.at[1], down1), (h_unpatch.at[1], unpatch1), (h_deal, deal),
    ]
    loads = [
        pltpu.make_async_copy(src, dst, load_sem.at[i]) for i, (src, dst) in enumerate(plan)
    ]
    for load in loads:
        load.start()

    def in_group(k):
        peer = lax.rem(me + k, GROUP)
        return peer, {"gz": peer // NY, "gy": plane * NY + lax.rem(peer, NY)}

    def in_other_plane(k):
        return {"gy": (1 - plane) * NY + lax.rem(y + k, NY)}

    barrier = pltpu.get_barrier_semaphore()
    for k in range(NY):
        pl.semaphore_signal(
            barrier, inc=1, device_id=in_other_plane(k), device_id_type=MESH_ID
        )

    @pl.loop(1, GROUP)
    def _(k):
        _, where = in_group(k)
        pl.semaphore_signal(barrier, inc=1, device_id=where, device_id_type=MESH_ID)

    def remote(src, dst, send, recv, where):
        return pltpu.make_async_remote_copy(
            src_ref=src, dst_ref=dst, send_sem=send, recv_sem=recv,
            device_id=where, device_id_type=MESH_ID,
        )

    for g in range(4):
        strips[g] = noisy[:, 128 * g : 128 * g + 128]
        for part in range(2):
            rows = [strips[g, pl.ds(8 * part + i, 16, stride=16), :] for i in range(8)]
            for i, block in enumerate(exchange_blocks(rows, 16)):
                high = block.astype(bf16)
                at = slice((8 * g + i) * 16, (8 * g + i) * 16 + 16)
                cut[at, 128 * part : 128 * part + 128] = high
                cut[at, 256 + 128 * part : 384 + 128 * part] = (
                    block - high.astype(f32)
                ).astype(bf16)
    loads[0].wait()
    own_src[...] = dot(cast[...], cut[...]).astype(bf16).reshape(GY, 64, 512)

    pl.semaphore_wait(barrier, GROUP - 1 + NY)
    peers = []
    for k in range(1, GY):
        peer = lax.rem(gy + k, GY)
        where = {"gy": peer}
        flip = lax.rem(peer + NY, GY)
        peers.append((peer, where))
        remote(own_src.at[peer], own_dst.at[gy], send_sem.at[0], recv_sem.at[0], where).start()
        remote(
            own_src.at[flip, :, pl.ds(0, 256)], oth_dst.at[gy], send_sem.at[1], recv_sem.at[1],
            where,
        ).start()
    own_dst[gy] = own_src[gy]
    oth_dst[gy] = own_src[lax.rem(gy + NY, GY), :, 0:256]

    for s in range(2):
        for g in range(4):
            part = noisy[128 * s : 128 * s + 128, 128 * g : 128 * g + 128].T
            relay_src[4 * g : 4 * g + 4, :, 128 * s : 128 * s + 128] = part.reshape(4, 32, 128)

    @pl.loop(1, GZ)
    def _(k):
        peer = lax.rem(gz + k, GZ)
        remote(
            relay_src.at[peer], relay_dst.at[gz], send_sem.at[2], recv_sem.at[2], {"gz": peer}
        ).start()

    relay_dst[gz] = relay_src[gz]

    for a in range(12):
        wide[a, :, 0:64] = measured[a] if a < 8 else cap[a - 8].astype(f32)
        quarter = [wide[a, pl.ds(q, 8, stride=4), :] for q in range(4)]
        for r in range(2):
            cells[a, 8 * r : 8 * r + 8, :] = jnp.concatenate(
                [v[:, 32 * r : 32 * r + 32] for v in quarter], axis=1
            )

    for load in loads[1:9]:
        load.wait()
    unpatch0[...] = dot(unpatch0[...], swap[...]).astype(bf16)

    def gather(dst, src, s, r, count):
        part = pl.ds(0, count)
        del src
        pltpu.make_async_copy(dst.at[part], dst.at[part], recv_sem.at[r]).wait()

    gather(own_dst, None, 0, 0, GY - 1)
    gather(oth_dst, None, 1, 1, GY - 1)
    arrived = own_dst[...].reshape(GY * 64, 512)
    tok[...] = dot(order[...], arrived[:, :256]).astype(bf16)
    low[...] = dot(order[...], arrived[:, 256:]).astype(bf16)
    gain0 = gains.at[0]

    @pl.loop(0, 2)
    def _(i):
        at = pl.ds(pl.multiple_of(i * 256, 256), 256)
        first = dot(tok[at, :], patch0[...]) + feat[...]
        hidden[at, :] = first
        normed = norm(first, gain0[0:1, :])
        queries[at, :] = (dot(normed, qkv0[:, :D]).astype(bf16) * 0.125).astype(bf16)
        pairs[at, :] = dot(normed, qkv0[:, D:]).astype(bf16)

    @pl.loop(0, 2)
    def _(i):
        part = oth_dst[pl.ds(i * 4, 4)].reshape(256, 256)
        normed = norm(dot(part, patch0[...]) + feat[...], gain0[0:1, :])
        at = pl.ds(pl.multiple_of(HALF + i * 256, 256), 256)
        pairs[at, :] = dot(normed, qkv0[:, D:]).astype(bf16)

    partner = in_other_plane(0)
    left = lax.broadcasted_iota(jnp.int32, (CHUNK, 128), 1) < 64

    @pl.loop(0, PARTS)
    def _(i):
        at = pl.ds(pl.multiple_of(i * CHUNK, CHUNK), CHUNK)
        attended = attention(queries[at, :], pairs[:, :D], pairs[:, D:], left)
        normed = tail(hidden[at, :], attended, out0, up0, down0, gain0)
        net = dot(unpatch0[...], normed, (((0,), (1,)), ((), ())))
        value = dot(swap[...], tok[at, :], NT) + dot(swap[...], low[at, :], NT)
        first = (value - scal[0] * net) * scal[1]
        guess[:, at] = first
        guess16[i] = first.astype(bf16)
        remote(
            guess16.at[i], guess_dst.at[i], pair_send.at[i], pair_recv.at[i], partner
        ).start()

    for load in loads[9:13]:
        load.wait()
    half_rows = pl.ds(pl.multiple_of(plane * HALF, HALF), HALF)
    side_rows = pl.ds(pl.multiple_of((1 - plane) * HALF, HALF), HALF)
    mine = jnp.concatenate([guess16[i] for i in range(PARTS)], axis=1)
    for c in range(4):
        at = slice(512 * c, 512 * c + 512)
        summed[:, at] = dot(mine, coarse[half_rows, at])
    for i in range(PARTS):
        remote(
            guess16.at[i], guess_dst.at[i], pair_send.at[i], pair_recv.at[i], partner
        ).wait()
    theirs = jnp.concatenate([guess_dst[i] for i in range(PARTS)], axis=1)
    for c in range(4):
        at = slice(256 * c, 256 * c + 256)
        im = slice(1024 + 256 * c, 1280 + 256 * c)
        real = summed[:, at] + dot(theirs, coarse[side_rows, at])
        imag = summed[:, im] + dot(theirs, coarse[side_rows, im])
        t_re, t_im = twist[0, :, at], twist[1, :, at]
        turned[0:256, at] = (real * t_re - imag * t_im).astype(bf16)
        turned[256:512, at] = (real * t_im + imag * t_re).astype(bf16)

    @pl.loop(0, 4)
    def _(i):
        block = lax.rem(i + gz // 4, 4)
        res = dot(fine[pl.ds(pl.multiple_of(block * 64, 64), 64), :], turned[...])
        for c in range(8):
            spread[pl.ds(c, 64, stride=8), :] = res[:, 128 * c : 128 * c + 128]
        line_src[pl.ds(block * 16, 16)] = spread[...].astype(bf16).reshape(16, 2, 16, 128)

        @pl.loop(0, 16)
        def _(j):
            peer = block * 16 + j

            @pl.when(peer != me)
            def _():
                where = {"gz": peer // NY, "gy": plane * NY + lax.rem(peer, NY)}
                remote(
                    line_src.at[peer], line_dst.at[me], send_sem.at[3], recv_sem.at[3], where
                ).start()

    line_dst[me] = line_src[me]

    angle = cells[8:12] * (2.0 * math.pi / NZ)
    w_re, w_im = jnp.cos(angle), -jnp.sin(angle)
    turns = lax.rem(cells[8:12].astype(jnp.int32) * me, NZ).astype(f32) * (2.0 * math.pi / NZ)
    first_re, first_im = jnp.cos(turns), jnp.sin(turns)
    gather(line_dst, None, 3, 3, GROUP - 1)

    def pick(i, state):
        p_re, p_im = state
        z = NZ - 1 - i
        x_re, x_im = line_dst[z, 0].astype(f32), line_dst[z, 1].astype(f32)
        return (
            p_re * w_re - p_im * w_im + x_re[None],
            p_re * w_im + p_im * w_re + x_im[None],
        )

    zero = jnp.zeros_like(w_re)
    p_re, p_im = lax.fori_loop(0, NZ, pick, (zero, zero), unroll=8)
    scale = 1.0 / math.sqrt(NZ)
    want = cells[0:8].reshape(4, 2, 16, 128)
    r_re = (want[:, 0] - p_re * scale) * scale
    r_im = (want[:, 1] - p_im * scale) * scale
    state = (r_re * first_re - r_im * first_im, r_re * first_im + r_im * first_re)

    def put(ref, z, state):
        t_re, t_im = state
        ref[z, 0] = (t_re[0] + t_re[1] + t_re[2] + t_re[3]).astype(bf16)
        ref[z, 1] = (t_im[0] + t_im[1] + t_im[2] + t_im[3]).astype(bf16)
        return (t_re * w_re + t_im * w_im, t_im * w_re - t_re * w_im)

    state = put(fix_dst, me, state)

    def expand(k, state):
        z, where = in_group(k)
        state = put(fix_src, z, state)
        remote(fix_src.at[z], fix_dst.at[me], send_sem.at[4], recv_sem.at[4], where).start()
        return state

    lax.fori_loop(1, GROUP, expand, state)

    gather(fix_dst, None, 4, 4, GROUP - 1)
    spread2[...] = fix_dst[...].reshape(GROUP * 32, 128).astype(f32)
    for c in range(4):
        at = slice(c * 256, c * 256 + 256)
        block = jnp.concatenate(
            [spread2[pl.ds(2 * c + k, 256, stride=8), :].astype(bf16) for k in range(2)], axis=1
        )
        res = dot(fine_t[...], block)
        real, imag = res[:256], res[256:]
        t_re, t_im = twist[0, :, at], twist[1, :, at]
        turned2[:, at] = (real * t_re + imag * t_im).astype(bf16)
        turned2[:, 1024 + c * 256 : 1280 + c * 256] = (imag * t_re - real * t_im).astype(bf16)
    for c in range(2):
        rows = pl.ds(pl.multiple_of((1 - plane) * HALF + c * 256, 256), 256)
        back_src[c] = dot(turned2[...], coarse[rows, :], NT).astype(bf16)
        remote(
            back_src.at[c], back_dst.at[c], pair_send.at[PARTS + c], pair_recv.at[PARTS + c],
            partner,
        ).start()
    for c in range(2):
        rows = pl.ds(pl.multiple_of(plane * HALF + c * 256, 256), 256)
        at = slice(c * 256, c * 256 + 256)
        blended[:, at] = guess[:, at] + dot(turned2[...], coarse[rows, :], NT)
    for c in range(2):
        at = slice(c * 256, c * 256 + 256)
        remote(
            back_src.at[c], back_dst.at[c], pair_send.at[PARTS + c], pair_recv.at[PARTS + c],
            partner,
        ).wait()
        blended[:, at] = blended[:, at] + back_dst[c].astype(f32)

    def send_columns(src, dst, which):
        @pl.loop(1, GROUP)
        def _(k):
            peer, where = in_group(k)
            remote(
                src.at[peer], dst.at[me], send_sem.at[which], recv_sem.at[which], where
            ).start()

    for q in range(4):
        for g in range(4):
            rows = [
                blended[q * 64 + r * 16 : q * 64 + r * 16 + 16, 128 * g : 128 * g + 128]
                for r in range(4)
            ]
            for i, block in enumerate(exchange_blocks(rows, 32)):
                high = block.astype(bf16)
                col_src[(4 * g + i) * 4 + q] = high
                rest_src[(4 * g + i) * 4 + q] = (block - high.astype(f32)).astype(bf16)
    send_columns(col_src, col_dst, 5)
    send_columns(rest_src, rest_dst, 6)
    col_dst[me] = col_src[me]
    rest_dst[me] = rest_src[me]

    for load in loads[13:]:
        load.wait()
    patch1[...] = dot(swap[...], patch1[...]).astype(bf16)
    unpatch1[...] = dot(unpatch1[...], swap[...]).astype(bf16)
    gather(col_dst, None, 5, 5, GROUP - 1)
    gain1 = gains.at[1]
    for zb in range(4):
        pix = col_dst[zb * 16 : zb * 16 + 16].reshape(256, 128)
        first = dot(pix, patch1[...], TN) + feat[...]
        for x in range(4):
            hidden[x * 128 + zb * 32 : x * 128 + zb * 32 + 32, :] = first[32 * x : 32 * x + 32, :]
    left1 = lax.broadcasted_iota(jnp.int32, (128, 128), 1) < 64

    @pl.loop(0, 4)
    def _(x):
        at = pl.ds(pl.multiple_of(128 * x, 128), 128)
        normed = norm(hidden[at, :], gain1[0:1, :])
        projected = dot(normed, qkv1[...]).astype(bf16)
        scaled = (projected[:, :D] * 0.125).astype(bf16)
        attended = attention(scaled, projected[:, D : 2 * D], projected[:, 2 * D :], left1)
        normed = tail(hidden[at, :], attended, out1, up1, down1, gain1)
        for zb in range(4):
            last[pl.ds(pl.multiple_of(zb * 128 + 32 * x, 32), 32), :] = normed[
                32 * zb : 32 * zb + 32, :
            ]

    gather(rest_dst, None, 6, 6, GROUP - 1)
    for j in range(4):
        rows = slice(128 * j, 128 * j + 128)
        moved = dot(deal[rows, :], last[...]).astype(bf16)
        value = scal[0] * dot(moved, unpatch1[...])
        for zb in range(4):
            for ref in (col_dst, rest_dst):
                pix = ref[zb * 16 : zb * 16 + 16].reshape(256, 128)
                value = value + dot(deal[rows, 128 * zb : 128 * zb + 128], pix, NT)
        final_src[2 * j : 2 * j + 2] = value.reshape(2, 64, 256)
    for peer, where in peers:
        remote(
            final_src.at[peer], final_dst.at[gy], send_sem.at[7], recv_sem.at[7], where
        ).start()
    final_dst[gy] = final_src[gy]

    def drain(src, which, count):
        part = pl.ds(0, count)
        pltpu.make_async_copy(src.at[part], src.at[part], send_sem.at[which]).wait()

    drain(own_src, 0, GY - 1)
    drain(oth_dst, 1, GY - 1)
    drain(relay_src, 2, GZ - 1)
    drain(line_src, 3, GROUP - 1)
    drain(fix_src, 4, GROUP - 1)
    drain(col_src, 5, GROUP - 1)
    drain(rest_src, 6, GROUP - 1)
    drain(final_src, 7, GY - 1)
    gather(relay_dst, None, 2, 2, GZ - 1)
    gather(final_dst, None, 7, 7, GY - 1)


def finish_kernel(coef, final, relay, noise, previous, estimate):
    row = lax.broadcasted_iota(jnp.int32, (8, 128), 0) < 4
    a, b, c = coef[0], coef[1], coef[2]
    for zb in range(4):
        for g in range(4):
            at = slice(8 * g, 8 * g + 8)
            for part in range(2):
                lanes = slice(128 * part, 128 * part + 128)
                blocks = []
                for yb in range(4):
                    base = 8 * ((zb * 4 + yb) // 2)
                    one = final[2 * g, base : base + 8, lanes]
                    two = final[2 * g + 1, base : base + 8, lanes]
                    if yb % 2 == 0:
                        blocks.append(jnp.where(row, one, pltpu.roll(two, 4, axis=0)))
                    else:
                        blocks.append(jnp.where(row, pltpu.roll(one, 4, axis=0), two))
                for i, block in enumerate(exchange_blocks(blocks, 16)):
                    for h in range(2):
                        z = zb * 16 + part * 8 + h * 4 + i
                        value = block[:, 64 * h : 64 * h + 64]
                        s = z % 4
                        old = relay[z // 4, at, 64 * s : 64 * s + 64]
                        estimate[z, at, :] = value
                        previous[z, at, :] = a * value + b * old + c * noise[z, at, :]


def local(
    noisy, noise, timestep, measured, cap_index, w_patch, w_qkv, w_out, w_up, w_down, w_unpatch,
    norm_gain,
):
    moment = timestep[0].astype(f32)
    signal_now = cumulative_alpha(moment)
    signal_prev = cumulative_alpha(moment - STRIDE)
    root_signal = jnp.sqrt(signal_now)
    root_noise = jnp.sqrt(1.0 - signal_now)
    features = time_features(moment)[None]
    scal = jnp.stack([root_noise, 1.0 / root_signal])
    toward = jnp.sqrt(
        (1.0 - signal_prev) * signal_now * (1.0 / signal_prev - 1.0) / (1.0 - signal_now)
    )
    spread = jnp.sqrt((1.0 - signal_prev) / (1.0 - signal_now) * (1.0 - signal_now / signal_prev))
    coef = jnp.stack(
        [jnp.sqrt(signal_prev) - toward * root_signal / root_noise, toward / root_noise, spread]
    )
    vmem = pl.BlockSpec(memory_space=pltpu.VMEM)
    smem = pl.BlockSpec(memory_space=pltpu.SMEM)
    anywhere = pl.BlockSpec(memory_space=pl.ANY)
    V = pltpu.VMEM
    weights = lambda: [
        V((PIX, D), bf16), V((D, 3 * D), bf16), V((D, D), bf16), V((D, FF), bf16),
        V((FF, D), bf16), V((D, PIX), bf16),
    ]
    final, relay = pl.pallas_call(
        step_kernel,
        out_shape=(
            jax.ShapeDtypeStruct((GY, 64, 256), f32),
            jax.ShapeDtypeStruct((GZ, 32, 256), f32),
        ),
        in_specs=[smem] + [vmem] * 5 + [anywhere] * 14,
        out_specs=(vmem, vmem),
        scratch_shapes=weights() + weights() + [
            V((1024, 2048), bf16), V((2, 256, 1024), f32), V((256, 512), bf16),
            V((512, 256), bf16), V((512, 512), bf16), V((256, 256), bf16),
            V((512, 512), bf16), V((512, 512), bf16),
            V((4, 256, 128), f32), V((12, 32, 128), f32),
            V((512, 512), bf16), V((GY, 64, 512), bf16), V((GY, 64, 512), bf16),
            V((GY, 64, 256), bf16), V((GZ, 32, 256), f32),
            V((HALF, PIX), bf16), V((HALF, PIX), bf16), V((HALF, D), f32), V((HALF, D), bf16),
            V((2 * HALF, 2 * D), bf16), V((PIX, HALF), f32), V((PARTS, PIX, CHUNK), bf16),
            V((PARTS, PIX, CHUNK), bf16),
            V((PIX, 2048), f32), V((512, 1024), bf16), V((512, 128), f32),
            V((GROUP, 2, 16, 128), bf16), V((GROUP, 2, 16, 128), bf16),
            V((12, 16, 128), f32), V((GROUP, 2, 16, 128), bf16), V((GROUP, 2, 16, 128), bf16),
            V((PIX, 2048), bf16), V((GROUP * 32, 128), f32), V((2, PIX, 256), bf16),
            V((2, PIX, 256), bf16), V((PIX, HALF), f32),
            V((GROUP, 16, 128), bf16), V((GROUP, 16, 128), bf16),
            V((GROUP, 16, 128), bf16), V((GROUP, 16, 128), bf16),
            V((512, D), bf16), V((GY, 64, 256), f32),
            pltpu.SemaphoreType.DMA((20,)), pltpu.SemaphoreType.DMA((8,)),
            pltpu.SemaphoreType.DMA((8,)), pltpu.SemaphoreType.DMA((PARTS + 2,)),
            pltpu.SemaphoreType.DMA((PARTS + 2,)),
        ],
        compiler_params=pltpu.CompilerParams(
            collective_id=0, has_side_effects=True, vmem_limit_bytes=56 * MIB
        ),
    )(
        scal, features, norm_gain, noisy.reshape(256, LAT), measured.reshape(8, 32, 64), cap_index,
        w_patch, w_qkv, w_out, w_up, w_down, w_unpatch, *(jnp.asarray(t) for t in tables()),
    )
    shape = jax.ShapeDtypeStruct((NZ, 32, 64), f32)
    previous, estimate = pl.pallas_call(
        finish_kernel,
        out_shape=(shape, shape),
        in_specs=[smem] + [vmem] * 3,
        out_specs=(vmem, vmem),
        compiler_params=pltpu.CompilerParams(vmem_limit_bytes=32 * MIB),
    )(coef, final, relay, noise.transpose(0, 2, 1))
    return (previous.transpose(0, 2, 1), estimate.transpose(0, 2, 1))


def solution(mesh):
    placed = (
        P("gz", "gy", None),
        P(None, "gy", "gz"),
        P(),
        P(None, None, "gz", "gy"),
        P(None, "gz", "gy"),
    ) + (P(),) * 7
    return jax.shard_map(
        local,
        mesh=mesh,
        in_specs=placed,
        out_specs=(P(None, "gy", "gz"), P(None, "gy", "gz")),
        check_vma=False,
    )
```

profile of v0, /device:TPU:1, one launch (start us, length us, event | category | flops | bytes accessed | tf_op | source)
XLA Modules:
  0.0 125.3 jit_solution(8926482532190968148)
XLA Ops:
  1.9 0.1 pad_maximum_fusion.1.coef
  2.0 0.6 pad_maximum_fusion.2.refs_0_
  2.7 0.1 pad_maximum_fusion
  2.8 0.6 broadcast_in_dim.3.refs_1_
  3.4 1.3 %copy.22.refs_2_ = f32[2,3,384]{2,1,0:T(4,128)} copy(f32[2,3,384]{2,0,1:T(2,128)} %param.31) | data formatting | bytes 18432 | tf_op args[11]
  4.7 0.0 copy-start
  4.7 111.0 %shard_map.203 = (f32[8,64,256]{2,1,0:T(8,128)}, f32[16,32,256]{2,1,0:T(8,128)}) custom-call(f32[2]{0:T(128)} %pad_maximum_fusion.2.refs_0_, f32[1,384]{1,0:T(1,128)} %broadcast_in_dim.3.refs_1_, f32[2,3,384]{2,1,0:T(4,128)} %copy.22.refs_2_, f32[256,512]{1,0:T(8,128)} %bitcast.12, f32[8,32,64]{2,1,0:T(8,128)} %bitcast.13, s32[4,32,64]{2,1,0:T(8,128)} %refs_5_.1, ...), custom_call_target="tpu_custom_call" | custom-call | tf_op jit(solution)/shard_map/pallas_call | solution.py:571
  115.7 0.0 copy-done
  115.7 0.0 copy-start.1
  115.7 1.0 copy-done.1
  116.7 0.0 copy-start.2
  116.7 1.0 copy-done.2
  117.8 7.6 %shard_map.204 = (f32[64,32,64]{2,1,0:T(8,128)}, f32[64,32,64]{2,1,0:T(8,128)}) custom-call(f32[3]{0:T(128)S(1)} %pad_maximum_fusion.1.coef, f32[8,64,256]{2,1,0:T(8,128)S(1)} %copy-done.1, f32[16,32,256]{2,1,0:T(8,128)S(1)} %copy-done.2, f32[64,32,64]{2,1,0:T(8,128)S(1)} %bitcast.11), custom_call_target="tpu_custom_call" | custom-call | tf_op jit(solution)/shard_map/pallas_call | solution.py:609
  (1 shorter events, 0.0 us)
Async XLA Ops:
  4.7 111.0 %copy-start = (f32[64,64,32]{1,2,0:T(8,128)S(1)}, f32[64,64,32]{1,2,0:T(8,128)}, u32[]{:S(2)}) copy-start(f32[64,64,32]{1,2,0:T(8,128)} %param.21) | copy-start | bytes 1572868
  115.7 1.0 copy-start.1
  116.7 1.0 copy-start.2
where the time goes:
time: 126 us; the launch traced here: 125 us
  Pallas kernels  119 us (94%)
  local copies, waits for them, and re-layouts  3.95 us (3%)
  between operations  1.97 us (2%)
    pallas_call x1, Pallas kernels, local(): pl.pallas_call(step_kernel, out_shape=(jax.ShapeDtypeStruct((GY, 64, 256)...  111 us
    pallas_call x1, Pallas kernels, local(): pl.pallas_call(finish_kernel, out_shape=(shape, shape), in_specs=[smem] +...  7.55 us
    unnamed x7, local copies, waits for them, and re-layouts  3.38 us

commit v1 on v0

--- a/solution.py
+++ b/solution.py
@@ -70,12 +70,14 @@
         for s in range(4):
             for yb in range(4):
                 cast[(xb % 2) * 256 + s * 64 + (xb // 2) * 4 + yb, xb * 16 + s * 4 + yb] = 1.0
-    deal = np.zeros((512, 512), np.float32)
-    for zb in range(4):
-        for x in range(4):
+    deal = np.zeros((256, 256), np.float32)
+    spill = np.zeros((2, 256, 512), np.float32)
+    for x in range(4):
+        for zb in range(4):
             for yb in range(32):
-                row = (yb // 4) * 64 + zb * 16 + (yb % 4) * 4 + x
-                deal[row, zb * 128 + x * 32 + yb] = 1.0
+                row = (yb // 4) * 32 + (x % 2) * 16 + zb * 4 + yb % 4
+                deal[row, (x % 2) * 128 + zb * 32 + yb] = 1.0
+                spill[x // 2, row, zb * 128 + x * 32 + yb] = 1.0
     return (
         to_bf(coarse),
         twist.astype(np.float32),
@@ -85,6 +87,7 @@
         to_bf(swap),
         to_bf(cast),
         to_bf(deal),
+        to_bf(spill),
     )
 
 
@@ -151,37 +154,38 @@
     return jnp.concatenate(outs, axis=1)
 
 
-def tail(hidden, attended, w_out, w_up, w_down, gains):
+def tail(hidden, attended, w_out, w_up, w_down, gain1, gain2):
     hidden = hidden + dot(attended, w_out[...])
-    normed = norm(hidden, gains[1:2, :])
-    inner = gelu(dot(normed, w_up[...])).astype(bf16)
+    inner = gelu(dot(norm(hidden, gain1), w_up[...])).astype(bf16)
     hidden = hidden + dot(inner, w_down[...])
-    return norm(hidden, gains[2:3, :])
-
-
-CHUNK = 128
-PARTS = HALF // CHUNK
+    return norm(hidden, gain2)
+
+
+PARTS = 4
+CHUNK = HALF // PARTS
 
 
 def step_kernel(*refs):
     (
-        scal, feat, gains, noisy, measured, cap,
+        consts, gains, noisy, noise, measured, cap,
         h_patch, h_qkv, h_out, h_up, h_down, h_unpatch,
-        h_coarse, h_twist, h_fine, h_fine_t, h_order, h_swap, h_cast, h_deal,
-        final_dst, relay_dst,
+        h_coarse, h_twist, h_fine, h_fine_t, h_order, h_swap, h_cast, h_deal, h_spill,
+        previous, estimate,
         patch0, qkv0, out0, up0, down0, unpatch0,
         patch1, qkv1, out1, up1, down1, unpatch1,
-        coarse, twist, fine, fine_t, order, swap, cast, deal,
-        strips, wide, cut, own_src, own_dst, oth_dst, relay_src,
-        tok, low, hidden, queries, pairs, guess, guess16, guess_dst,
+        coarse, twist, fine, fine_t, order, swap, cast, deal, spill,
+        strips, wide, cut, high_src, low_src, own_dst, oth_dst, low_dst, relay_src, relay_dst,
+        tok, hidden, queries, pairs, guess, guess16, guess_dst,
         summed, turned, spread, line_src, line_dst,
         cells, fix_src, fix_dst, turned2, spread2, back_src, back_dst, blended,
-        col_src, col_dst, rest_src, rest_dst, last, final_src,
-        load_sem, send_sem, recv_sem, pair_send, pair_recv,
+        col_src, col_dst, final_src, final_dst,
+        load_sem, send_sem, recv_sem, pair_send, pair_recv, ready,
     ) = refs
     gz, gy = lax.axis_index("gz"), lax.axis_index("gy")
     plane, y = gy // NY, gy % NY
     me = gz * NY + y
+    feat = consts[0:1, :]
+    root_noise, inv_signal = consts[1:2, 0:1], consts[1:2, 1:2]
 
     plan = [
         (h_cast, cast), (h_swap, swap), (h_order, order), (h_patch.at[0], patch0),
@@ -190,6 +194,7 @@
         (h_fine.at[plane], fine), (h_fine_t.at[plane], fine_t),
         (h_patch.at[1], patch1), (h_qkv.at[1], qkv1), (h_out.at[1], out1), (h_up.at[1], up1),
         (h_down.at[1], down1), (h_unpatch.at[1], unpatch1), (h_deal, deal),
+        (h_spill, spill),
     ]
     loads = [
         pltpu.make_async_copy(src, dst, load_sem.at[i]) for i, (src, dst) in enumerate(plan)
@@ -205,15 +210,14 @@
         return {"gy": (1 - plane) * NY + lax.rem(y + k, NY)}
 
     barrier = pltpu.get_barrier_semaphore()
-    for k in range(NY):
+    for k in range(1, GY):
         pl.semaphore_signal(
-            barrier, inc=1, device_id=in_other_plane(k), device_id_type=MESH_ID
+            barrier, inc=1, device_id={"gy": lax.rem(gy + k, GY)}, device_id_type=MESH_ID
         )
-
-    @pl.loop(1, GROUP)
-    def _(k):
-        _, where = in_group(k)
-        pl.semaphore_signal(barrier, inc=1, device_id=where, device_id_type=MESH_ID)
+    for k in range(1, GZ):
+        pl.semaphore_signal(
+            barrier, inc=1, device_id={"gz": lax.rem(gz + k, GZ)}, device_id_type=MESH_ID
+        )
 
     def remote(src, dst, send, recv, where):
         return pltpu.make_async_remote_copy(
@@ -233,22 +237,29 @@
                     block - high.astype(f32)
                 ).astype(bf16)
     loads[0].wait()
-    own_src[...] = dot(cast[...], cut[...]).astype(bf16).reshape(GY, 64, 512)
-
-    pl.semaphore_wait(barrier, GROUP - 1 + NY)
+    sorted_rows = dot(cast[...], cut[...]).astype(bf16).reshape(GY, 64, 512)
+    high_src[...] = sorted_rows[:, :, :256]
+    low_src[...] = sorted_rows[:, :, 256:]
+
+    pl.semaphore_wait(barrier, GY - 1 + GZ - 1)
     peers = []
     for k in range(1, GY):
         peer = lax.rem(gy + k, GY)
         where = {"gy": peer}
         flip = lax.rem(peer + NY, GY)
         peers.append((peer, where))
-        remote(own_src.at[peer], own_dst.at[gy], send_sem.at[0], recv_sem.at[0], where).start()
-        remote(
-            own_src.at[flip, :, pl.ds(0, 256)], oth_dst.at[gy], send_sem.at[1], recv_sem.at[1],
-            where,
-        ).start()
-    own_dst[gy] = own_src[gy]
-    oth_dst[gy] = own_src[lax.rem(gy + NY, GY), :, 0:256]
+        remote(high_src.at[flip], oth_dst.at[gy], send_sem.at[1], recv_sem.at[1], where).start()
+        remote(high_src.at[peer], own_dst.at[gy], send_sem.at[0], recv_sem.at[0], where).start()
+    for peer, where in peers:
+        remote(low_src.at[peer], low_dst.at[gy], send_sem.at[6], recv_sem.at[6], where).start()
+    for k in range(1, NY):
+        pl.semaphore_signal(
+            ready, inc=1, device_id={"gy": plane * NY + lax.rem(y + k, NY)},
+            device_id_type=MESH_ID,
+        )
+    own_dst[gy] = high_src[gy]
+    oth_dst[gy] = high_src[lax.rem(gy + NY, GY)]
+    low_dst[gy] = low_src[gy]
 
     for s in range(2):
         for g in range(4):
@@ -283,38 +294,30 @@
 
     gather(own_dst, None, 0, 0, GY - 1)
     gather(oth_dst, None, 1, 1, GY - 1)
-    arrived = own_dst[...].reshape(GY * 64, 512)
-    tok[...] = dot(order[...], arrived[:, :256]).astype(bf16)
-    low[...] = dot(order[...], arrived[:, 256:]).astype(bf16)
-    gain0 = gains.at[0]
-
-    @pl.loop(0, 2)
-    def _(i):
-        at = pl.ds(pl.multiple_of(i * 256, 256), 256)
-        first = dot(tok[at, :], patch0[...]) + feat[...]
-        hidden[at, :] = first
-        normed = norm(first, gain0[0:1, :])
-        queries[at, :] = (dot(normed, qkv0[:, :D]).astype(bf16) * 0.125).astype(bf16)
-        pairs[at, :] = dot(normed, qkv0[:, D:]).astype(bf16)
-
-    @pl.loop(0, 2)
-    def _(i):
-        part = oth_dst[pl.ds(i * 4, 4)].reshape(256, 256)
-        normed = norm(dot(part, patch0[...]) + feat[...], gain0[0:1, :])
-        at = pl.ds(pl.multiple_of(HALF + i * 256, 256), 256)
-        pairs[at, :] = dot(normed, qkv0[:, D:]).astype(bf16)
-
-    partner = in_other_plane(0)
-    left = lax.broadcasted_iota(jnp.int32, (CHUNK, 128), 1) < 64
-
-    @pl.loop(0, PARTS)
-    def _(i):
-        at = pl.ds(pl.multiple_of(i * CHUNK, CHUNK), CHUNK)
-        attended = attention(queries[at, :], pairs[:, :D], pairs[:, D:], left)
-        normed = tail(hidden[at, :], attended, out0, up0, down0, gain0)
-        net = dot(unpatch0[...], normed, (((0,), (1,)), ((), ())))
-        value = dot(swap[...], tok[at, :], NT) + dot(swap[...], low[at, :], NT)
-        first = (value - scal[0] * net) * scal[1]
+    tok[...] = dot(order[...], own_dst[...].reshape(HALF, 256)).astype(bf16)
+
+    def gain(m, r):
+        return gains[r, m : m + 1, :]
+
+    first = dot(tok[...], patch0[...]) + feat
+    hidden[...] = first
+    normed = norm(first, gain(0, 0))
+    queries[...] = (dot(normed, qkv0[:, :D]).astype(bf16) * 0.125).astype(bf16)
+    pairs[0:HALF, :] = dot(normed, qkv0[:, D:]).astype(bf16)
+    normed = norm(dot(oth_dst[...].reshape(HALF, 256), patch0[...]) + feat, gain(0, 0))
+    pairs[HALF:, :] = dot(normed, qkv0[:, D:]).astype(bf16)
+
+    partner = {"gy": (1 - plane) * NY + y}
+    left = lax.broadcasted_iota(jnp.int32, (HALF, 128), 1) < 64
+    attended = attention(queries[...], pairs[:, :D], pairs[:, D:], left)
+    queries[...] = tail(hidden[...], attended, out0, up0, down0, gain(0, 1), gain(0, 2))
+    gather(low_dst, None, 6, 6, GY - 1)
+    low = dot(order[...], low_dst[...].reshape(HALF, 256)).astype(bf16)
+    summed[:, 0:HALF] = dot(swap[...], tok[...], NT) + dot(swap[...], low, NT)
+    for i in range(PARTS):
+        at = slice(i * CHUNK, i * CHUNK + CHUNK)
+        net = dot(unpatch0[...], queries[at, :], (((0,), (1,)), ((), ())))
+        first = (summed[:, at] - root_noise * net) * inv_signal
         guess[:, at] = first
         guess16[i] = first.astype(bf16)
         remote(
@@ -342,6 +345,8 @@
         t_re, t_im = twist[0, :, at], twist[1, :, at]
         turned[0:256, at] = (real * t_re - imag * t_im).astype(bf16)
         turned[256:512, at] = (real * t_im + imag * t_re).astype(bf16)
+
+    pl.semaphore_wait(ready, NY - 1)
 
     @pl.loop(0, 4)
     def _(i):
@@ -434,14 +439,6 @@
         ).wait()
         blended[:, at] = blended[:, at] + back_dst[c].astype(f32)
 
-    def send_columns(src, dst, which):
-        @pl.loop(1, GROUP)
-        def _(k):
-            peer, where = in_group(k)
-            remote(
-                src.at[peer], dst.at[me], send_sem.at[which], recv_sem.at[which], where
-            ).start()
-
     for q in range(4):
         for g in range(4):
             rows = [
@@ -449,97 +446,90 @@
                 for r in range(4)
             ]
             for i, block in enumerate(exchange_blocks(rows, 32)):
-                high = block.astype(bf16)
-                col_src[(4 * g + i) * 4 + q] = high
-                rest_src[(4 * g + i) * 4 + q] = (block - high.astype(f32)).astype(bf16)
-    send_columns(col_src, col_dst, 5)
-    send_columns(rest_src, rest_dst, 6)
+                col_src[(4 * g + i) * 4 + q] = block.astype(bf16)
+
+    @pl.loop(1, GROUP)
+    def _(k):
+        peer, where = in_group(k)
+        remote(col_src.at[peer], col_dst.at[me], send_sem.at[5], recv_sem.at[5], where).start()
+
     col_dst[me] = col_src[me]
-    rest_dst[me] = rest_src[me]
+
+    gather(relay_dst, None, 2, 2, GZ - 1)
+    c_est, c_old, c_new = consts[1:2, 2:3], consts[1:2, 3:4], consts[1:2, 4:5]
+
+    @pl.loop(0, GZ)
+    def _(i):
+        for z in range(4):
+            previous[4 * i + z] = (
+                c_old * relay_dst[i, :, 64 * z : 64 * z + 64] + c_new * noise[4 * i + z]
+            )
 
     for load in loads[13:]:
         load.wait()
     patch1[...] = dot(swap[...], patch1[...]).astype(bf16)
     unpatch1[...] = dot(unpatch1[...], swap[...]).astype(bf16)
     gather(col_dst, None, 5, 5, GROUP - 1)
-    gain1 = gains.at[1]
     for zb in range(4):
         pix = col_dst[zb * 16 : zb * 16 + 16].reshape(256, 128)
-        first = dot(pix, patch1[...], TN) + feat[...]
+        first = dot(pix, patch1[...], TN) + feat
         for x in range(4):
             hidden[x * 128 + zb * 32 : x * 128 + zb * 32 + 32, :] = first[32 * x : 32 * x + 32, :]
+    normed = norm(hidden[...], gain(1, 0))
+    queries[...] = (dot(normed, qkv1[:, :D]).astype(bf16) * 0.125).astype(bf16)
+    pairs[0:HALF, :] = dot(normed, qkv1[:, D:]).astype(bf16)
     left1 = lax.broadcasted_iota(jnp.int32, (128, 128), 1) < 64
-
-    @pl.loop(0, 4)
-    def _(x):
-        at = pl.ds(pl.multiple_of(128 * x, 128), 128)
-        normed = norm(hidden[at, :], gain1[0:1, :])
-        projected = dot(normed, qkv1[...]).astype(bf16)
-        scaled = (projected[:, :D] * 0.125).astype(bf16)
-        attended = attention(scaled, projected[:, D : 2 * D], projected[:, 2 * D :], left1)
-        normed = tail(hidden[at, :], attended, out1, up1, down1, gain1)
+    for p in range(2):
+        half = slice(256 * p, 256 * p + 256)
+        attended = []
+        for x in range(2):
+            at = slice(256 * p + 128 * x, 256 * p + 128 * x + 128)
+            attended.append(attention(queries[at, :], pairs[at, :D], pairs[at, D:], left1))
+        attended = jnp.concatenate(attended, axis=0)
+        normed = tail(hidden[half, :], attended, out1, up1, down1, gain(1, 1), gain(1, 2))
+        moved = dot(deal[...], normed).astype(bf16)
+        value = root_noise * dot(moved, unpatch1[...])
         for zb in range(4):
-            last[pl.ds(pl.multiple_of(zb * 128 + 32 * x, 32), 32), :] = normed[
-                32 * zb : 32 * zb + 32, :
-            ]
-
-    gather(rest_dst, None, 6, 6, GROUP - 1)
-    for j in range(4):
-        rows = slice(128 * j, 128 * j + 128)
-        moved = dot(deal[rows, :], last[...]).astype(bf16)
-        value = scal[0] * dot(moved, unpatch1[...])
-        for zb in range(4):
-            for ref in (col_dst, rest_dst):
-                pix = ref[zb * 16 : zb * 16 + 16].reshape(256, 128)
-                value = value + dot(deal[rows, 128 * zb : 128 * zb + 128], pix, NT)
-        final_src[2 * j : 2 * j + 2] = value.reshape(2, 64, 256)
-    for peer, where in peers:
-        remote(
-            final_src.at[peer], final_dst.at[gy], send_sem.at[7], recv_sem.at[7], where
-        ).start()
-    final_dst[gy] = final_src[gy]
+            pix = col_dst[zb * 16 : zb * 16 + 16].reshape(256, 128)
+            value = value + dot(spill[p, :, 128 * zb : 128 * zb + 128], pix, NT)
+        for h in range(2):
+            final_src[p, :, h] = value[:, 128 * h : 128 * h + 128].reshape(GY, 32, 128)
+        here = pl.ds(pl.multiple_of(gy * 64 + p * 32, 32), 32)
+        for peer, where in peers:
+            remote(
+                final_src.at[p, peer], final_dst.at[:, here, :], send_sem.at[7], recv_sem.at[7],
+                where,
+            ).start()
+        final_dst[:, here, :] = final_src[p, gy]
 
     def drain(src, which, count):
         part = pl.ds(0, count)
         pltpu.make_async_copy(src.at[part], src.at[part], send_sem.at[which]).wait()
 
-    drain(own_src, 0, GY - 1)
-    drain(oth_dst, 1, GY - 1)
+    drain(high_src, 0, GY - 1)
+    drain(high_src, 1, GY - 1)
+    drain(low_src, 6, GY - 1)
     drain(relay_src, 2, GZ - 1)
     drain(line_src, 3, GROUP - 1)
     drain(fix_src, 4, GROUP - 1)
     drain(col_src, 5, GROUP - 1)
-    drain(rest_src, 6, GROUP - 1)
-    drain(final_src, 7, GY - 1)
-    gather(relay_dst, None, 2, 2, GZ - 1)
-    gather(final_dst, None, 7, 7, GY - 1)
-
-
-def finish_kernel(coef, final, relay, noise, previous, estimate):
-    row = lax.broadcasted_iota(jnp.int32, (8, 128), 0) < 4
-    a, b, c = coef[0], coef[1], coef[2]
-    for zb in range(4):
-        for g in range(4):
-            at = slice(8 * g, 8 * g + 8)
-            for part in range(2):
-                lanes = slice(128 * part, 128 * part + 128)
-                blocks = []
-                for yb in range(4):
-                    base = 8 * ((zb * 4 + yb) // 2)
-                    one = final[2 * g, base : base + 8, lanes]
-                    two = final[2 * g + 1, base : base + 8, lanes]
-                    if yb % 2 == 0:
-                        blocks.append(jnp.where(row, one, pltpu.roll(two, 4, axis=0)))
-                    else:
-                        blocks.append(jnp.where(row, pltpu.roll(one, 4, axis=0), two))
+    done = final_dst.at[:, pl.ds(0, (GY - 1) * 64), :]
+    pltpu.make_async_copy(done, done, send_sem.at[7]).wait()
+    pltpu.make_async_copy(done, done, recv_sem.at[7]).wait()
+
+    for g in range(4):
+        at = slice(8 * g, 8 * g + 8)
+        for zb in range(4):
+            for h in range(2):
+                blocks = [
+                    final_dst[h, pl.ds(128 * g + zb * 4 + yb, 8, stride=16), :] for yb in range(4)
+                ]
                 for i, block in enumerate(exchange_blocks(blocks, 16)):
-                    for h in range(2):
-                        z = zb * 16 + part * 8 + h * 4 + i
-                        value = block[:, 64 * h : 64 * h + 64]
-                        s = z % 4
-                        old = relay[z // 4, at, 64 * s : 64 * s + 64]
+                    for part in range(2):
+                        z = zb * 16 + h * 8 + part * 4 + i
+                        value = block[:, 64 * part : 64 * part + 64]
                         estimate[z, at, :] = value
-                        previous[z, at, :] = a * value + b * old + c * noise[z, at, :]
+                        previous[z, at, :] = previous[z, at, :] + c_est * value
 
 
 def local(
@@ -551,39 +541,41 @@
     signal_prev = cumulative_alpha(moment - STRIDE)
     root_signal = jnp.sqrt(signal_now)
     root_noise = jnp.sqrt(1.0 - signal_now)
-    features = time_features(moment)[None]
-    scal = jnp.stack([root_noise, 1.0 / root_signal])
     toward = jnp.sqrt(
         (1.0 - signal_prev) * signal_now * (1.0 / signal_prev - 1.0) / (1.0 - signal_now)
     )
     spread = jnp.sqrt((1.0 - signal_prev) / (1.0 - signal_now) * (1.0 - signal_now / signal_prev))
-    coef = jnp.stack(
-        [jnp.sqrt(signal_prev) - toward * root_signal / root_noise, toward / root_noise, spread]
+    coefs = (
+        root_noise, 1.0 / root_signal, jnp.sqrt(signal_prev) - toward * root_signal / root_noise,
+        toward / root_noise, spread,
     )
+    place = lax.broadcasted_iota(jnp.int32, (1, D), 1)
+    row = jnp.zeros((1, D), f32)
+    for i, value in enumerate(coefs):
+        row = jnp.where(place == i, value, row)
+    consts = jnp.concatenate([time_features(moment)[None], row], axis=0)
     vmem = pl.BlockSpec(memory_space=pltpu.VMEM)
-    smem = pl.BlockSpec(memory_space=pltpu.SMEM)
     anywhere = pl.BlockSpec(memory_space=pl.ANY)
     V = pltpu.VMEM
     weights = lambda: [
         V((PIX, D), bf16), V((D, 3 * D), bf16), V((D, D), bf16), V((D, FF), bf16),
         V((FF, D), bf16), V((D, PIX), bf16),
     ]
-    final, relay = pl.pallas_call(
+    shape = jax.ShapeDtypeStruct((NZ, 32, 64), f32)
+    previous, estimate = pl.pallas_call(
         step_kernel,
-        out_shape=(
-            jax.ShapeDtypeStruct((GY, 64, 256), f32),
-            jax.ShapeDtypeStruct((GZ, 32, 256), f32),
-        ),
-        in_specs=[smem] + [vmem] * 5 + [anywhere] * 14,
+        out_shape=(shape, shape),
+        in_specs=[vmem] * 6 + [anywhere] * 15,
         out_specs=(vmem, vmem),
         scratch_shapes=weights() + weights() + [
             V((1024, 2048), bf16), V((2, 256, 1024), f32), V((256, 512), bf16),
             V((512, 256), bf16), V((512, 512), bf16), V((256, 256), bf16),
-            V((512, 512), bf16), V((512, 512), bf16),
-            V((4, 256, 128), f32), V((12, 32, 128), f32),
-            V((512, 512), bf16), V((GY, 64, 512), bf16), V((GY, 64, 512), bf16),
-            V((GY, 64, 256), bf16), V((GZ, 32, 256), f32),
-            V((HALF, PIX), bf16), V((HALF, PIX), bf16), V((HALF, D), f32), V((HALF, D), bf16),
+            V((512, 512), bf16), V((256, 256), bf16), V((2, 256, 512), bf16),
+            V((4, 256, 128), f32), V((12, 32, 128), f32), V((512, 512), bf16),
+            V((GY, 64, 256), bf16), V((GY, 64, 256), bf16), V((GY, 64, 256), bf16),
+            V((GY, 64, 256), bf16), V((GY, 64, 256), bf16),
+            V((GZ, 32, 256), f32), V((GZ, 32, 256), f32),
+            V((HALF, PIX), bf16), V((HALF, D), f32), V((HALF, D), bf16),
             V((2 * HALF, 2 * D), bf16), V((PIX, HALF), f32), V((PARTS, PIX, CHUNK), bf16),
             V((PARTS, PIX, CHUNK), bf16),
             V((PIX, 2048), f32), V((512, 1024), bf16), V((512, 128), f32),
@@ -592,27 +584,19 @@
             V((PIX, 2048), bf16), V((GROUP * 32, 128), f32), V((2, PIX, 256), bf16),
             V((2, PIX, 256), bf16), V((PIX, HALF), f32),
             V((GROUP, 16, 128), bf16), V((GROUP, 16, 128), bf16),
-            V((GROUP, 16, 128), bf16), V((GROUP, 16, 128), bf16),
-            V((512, D), bf16), V((GY, 64, 256), f32),
-            pltpu.SemaphoreType.DMA((20,)), pltpu.SemaphoreType.DMA((8,)),
+            V((2, GY, 2, 32, 128), f32), V((2, 512, 128), f32),
+            pltpu.SemaphoreType.DMA((21,)), pltpu.SemaphoreType.DMA((8,)),
             pltpu.SemaphoreType.DMA((8,)), pltpu.SemaphoreType.DMA((PARTS + 2,)),
-            pltpu.SemaphoreType.DMA((PARTS + 2,)),
+            pltpu.SemaphoreType.DMA((PARTS + 2,)), pltpu.SemaphoreType.REGULAR,
         ],
         compiler_params=pltpu.CompilerParams(
-            collective_id=0, has_side_effects=True, vmem_limit_bytes=56 * MIB
+            collective_id=0, has_side_effects=True, vmem_limit_bytes=58 * MIB
         ),
     )(
-        scal, features, norm_gain, noisy.reshape(256, LAT), measured.reshape(8, 32, 64), cap_index,
+        consts, norm_gain.transpose(1, 0, 2), noisy.reshape(256, LAT), noise.transpose(0, 2, 1),
+        measured.reshape(8, 32, 64), cap_index,
         w_patch, w_qkv, w_out, w_up, w_down, w_unpatch, *(jnp.asarray(t) for t in tables()),
     )
-    shape = jax.ShapeDtypeStruct((NZ, 32, 64), f32)
-    previous, estimate = pl.pallas_call(
-        finish_kernel,
-        out_shape=(shape, shape),
-        in_specs=[smem] + [vmem] * 3,
-        out_specs=(vmem, vmem),
-        compiler_params=pltpu.CompilerParams(vmem_limit_bytes=32 * MIB),
-    )(coef, final, relay, noise.transpose(0, 2, 1))
     return (previous.transpose(0, 2, 1), estimate.transpose(0, 2, 1))
 
 

time: 126 us -> 105 us (0.83)
  Pallas kernels: 119 us -> 98.8 us
    pallas_call x2 -> x1, Pallas kernels: 119 us -> 98.8 us  [local(): pl.pallas_call(step_kernel, out_shape=(shape, shape), in_specs=[vmem] * 6...]
    unnamed x7 -> x4, local copies, waits for them, and re-layouts: 3.38 us -> 3.32 us
where the time goes in v1:
time: 105 us
  Pallas kernels  98.8 us (94%)
  local copies, waits for them, and re-layouts  3.33 us (3%)
  between operations  1.97 us (2%)
    pallas_call x1, Pallas kernels, local(): pl.pallas_call(step_kernel, out_shape=(shape, shape), in_specs=[vmem] * 6...  98.8 us
    unnamed x4, local copies, waits for them, and re-layouts  3.32 us

profile of v1, /device:TPU:1, one launch (start us, length us, event | category | flops | bytes accessed | tf_op | source)
XLA Modules:
  0.0 104.8 jit_solution(10782571136612440228)
XLA Ops:
  2.0 0.1 pad_maximum_fusion.1
  2.1 0.6 pad_maximum_fusion.refs_0_
  2.7 98.8 %shard_map.212 = (f32[64,32,64]{2,1,0:T(8,128)}, f32[64,32,64]{2,1,0:T(8,128)}) custom-call(f32[2,384]{1,0:T(2,128)} %pad_maximum_fusion.refs_0_, f32[3,2,384]{2,1,0:T(2,128)} %bitcast.12, f32[256,512]{1,0:T(8,128)} %bitcast.10, f32[64,32,64]{2,1,0:T(8,128)} %bitcast.7, f32[8,32,64]{2,1,0:T(8,128)} %bitcast.11, s32[4,32,64]{2,1,0:T(8,128)} %refs_5_.1, ...), custom_call_target="tpu_custom_call" | custom-call | tf_op jit(solution)/shard_map/pallas_call | solution.py:565
  101.5 0.0 copy-start
  101.5 2.4 %copy.26 = f32[64,64,32]{1,2,0:T(8,128)} copy(f32[64,64,32]{1,2,0:T(8,128)} %bitcast.9) | data formatting | bytes 1048576
  103.9 0.0 copy-done
  103.9 1.0 copy.27
  (3 shorter events, 0.1 us)
Async XLA Ops:
  101.5 2.4 %copy-start = (f32[64,32,64]{2,1,0:T(8,128)S(1)}, f32[64,32,64]{2,1,0:T(8,128)}, u32[]{:S(2)}) copy-start(f32[64,32,64]{2,1,0:T(8,128)} %get-tuple-element.5) | copy-start | bytes 1572868

commit v2 on v1

--- a/solution.py
+++ b/solution.py
@@ -182,8 +182,11 @@
         load_sem, send_sem, recv_sem, pair_send, pair_recv, ready,
     ) = refs
     gz, gy = lax.axis_index("gz"), lax.axis_index("gy")
-    plane, y = gy // NY, gy % NY
-    me = gz * NY + y
+    col, plane = gz // 2, lax.rem(gz, 2)
+    mine = col * GY + gy
+    me = gz * NY + lax.rem(gy, NY)
+    keeps = plane == gy // NY
+    partner = {"gz": 2 * col + 1 - plane}
     feat = consts[0:1, :]
     root_noise, inv_signal = consts[1:2, 0:1], consts[1:2, 1:2]
 
@@ -202,28 +205,32 @@
     for load in loads:
         load.start()
 
-    def in_group(k):
-        peer = lax.rem(me + k, GROUP)
-        return peer, {"gz": peer // NY, "gy": plane * NY + lax.rem(peer, NY)}
-
-    def in_other_plane(k):
-        return {"gy": (1 - plane) * NY + lax.rem(y + k, NY)}
-
     barrier = pltpu.get_barrier_semaphore()
-    for k in range(1, GY):
-        pl.semaphore_signal(
-            barrier, inc=1, device_id={"gy": lax.rem(gy + k, GY)}, device_id_type=MESH_ID
-        )
-    for k in range(1, GZ):
-        pl.semaphore_signal(
-            barrier, inc=1, device_id={"gz": lax.rem(gz + k, GZ)}, device_id_type=MESH_ID
-        )
+    for core in range(2):
+        for k in range(1 - core, GY):
+            where = {"gz": 2 * col + lax.rem(plane + core, 2), "gy": lax.rem(gy + k, GY)}
+            pl.semaphore_signal(barrier, inc=1, device_id=where, device_id_type=MESH_ID)
+        for k in range(1, GZ // 2):
+            where = {"gz": 2 * lax.rem(col + k, GZ // 2) + core}
+            pl.semaphore_signal(barrier, inc=1, device_id=where, device_id_type=MESH_ID)
 
     def remote(src, dst, send, recv, where):
         return pltpu.make_async_remote_copy(
             src_ref=src, dst_ref=dst, send_sem=send, recv_sem=recv,
             device_id=where, device_id_type=MESH_ID,
         )
+
+    def send(src, dst, which, to_gz, to_gy):
+        here = jnp.logical_and(to_gz == gz, to_gy == gy)
+
+        @pl.when(here)
+        def _():
+            pltpu.make_async_copy(src, dst, recv_sem.at[which]).start()
+
+        @pl.when(jnp.logical_not(here))
+        def _():
+            where = {"gz": to_gz, "gy": to_gy}
+            remote(src, dst, send_sem.at[which], recv_sem.at[which], where).start()
 
     for g in range(4):
         strips[g] = noisy[:, 128 * g : 128 * g + 128]
@@ -241,37 +248,29 @@
     high_src[...] = sorted_rows[:, :, :256]
     low_src[...] = sorted_rows[:, :, 256:]
 
-    pl.semaphore_wait(barrier, GY - 1 + GZ - 1)
+    pl.semaphore_wait(barrier, 2 * GY - 1 + GZ - 2)
+
+    def send_patches(src, dst, which):
+        for k in range(NY):
+            slot = lax.rem(gy + k, NY)
+            for half in range(2):
+                send(
+                    src.at[half * NY + slot], dst.at[gy], which, 2 * col + half,
+                    plane * NY + slot,
+                )
+
+    send_patches(high_src, own_dst, 0)
     peers = []
     for k in range(1, GY):
         peer = lax.rem(gy + k, GY)
         where = {"gy": peer}
-        flip = lax.rem(peer + NY, GY)
         peers.append((peer, where))
-        remote(high_src.at[flip], oth_dst.at[gy], send_sem.at[1], recv_sem.at[1], where).start()
-        remote(high_src.at[peer], own_dst.at[gy], send_sem.at[0], recv_sem.at[0], where).start()
-    for peer, where in peers:
-        remote(low_src.at[peer], low_dst.at[gy], send_sem.at[6], recv_sem.at[6], where).start()
-    for k in range(1, NY):
-        pl.semaphore_signal(
-            ready, inc=1, device_id={"gy": plane * NY + lax.rem(y + k, NY)},
-            device_id_type=MESH_ID,
-        )
-    own_dst[gy] = high_src[gy]
-    oth_dst[gy] = high_src[lax.rem(gy + NY, GY)]
-    low_dst[gy] = low_src[gy]
+        pl.semaphore_signal(ready, inc=1, device_id=where, device_id_type=MESH_ID)
 
     for s in range(2):
         for g in range(4):
             part = noisy[128 * s : 128 * s + 128, 128 * g : 128 * g + 128].T
             relay_src[4 * g : 4 * g + 4, :, 128 * s : 128 * s + 128] = part.reshape(4, 32, 128)
-
-    @pl.loop(1, GZ)
-    def _(k):
-        peer = lax.rem(gz + k, GZ)
-        remote(
-            relay_src.at[peer], relay_dst.at[gz], send_sem.at[2], recv_sem.at[2], {"gz": peer}
-        ).start()
 
     relay_dst[gz] = relay_src[gz]
 
@@ -292,8 +291,18 @@
         del src
         pltpu.make_async_copy(dst.at[part], dst.at[part], recv_sem.at[r]).wait()
 
-    gather(own_dst, None, 0, 0, GY - 1)
-    gather(oth_dst, None, 1, 1, GY - 1)
+    gather(own_dst, None, 0, 0, GY)
+    swap_own = remote(own_dst, oth_dst, send_sem.at[1], recv_sem.at[1], partner)
+    swap_own.start()
+    send_patches(low_src, low_dst, 6)
+
+    @pl.loop(1, GZ)
+    def _(k):
+        peer = lax.rem(gz + k, GZ)
+        remote(
+            relay_src.at[peer], relay_dst.at[gz], send_sem.at[2], recv_sem.at[2], {"gz": peer}
+        ).start()
+
     tok[...] = dot(order[...], own_dst[...].reshape(HALF, 256)).astype(bf16)
 
     def gain(m, r):
@@ -304,14 +313,14 @@
     normed = norm(first, gain(0, 0))
     queries[...] = (dot(normed, qkv0[:, :D]).astype(bf16) * 0.125).astype(bf16)
     pairs[0:HALF, :] = dot(normed, qkv0[:, D:]).astype(bf16)
+    swap_own.wait()
     normed = norm(dot(oth_dst[...].reshape(HALF, 256), patch0[...]) + feat, gain(0, 0))
     pairs[HALF:, :] = dot(normed, qkv0[:, D:]).astype(bf16)
 
-    partner = {"gy": (1 - plane) * NY + y}
     left = lax.broadcasted_iota(jnp.int32, (HALF, 128), 1) < 64
     attended = attention(queries[...], pairs[:, :D], pairs[:, D:], left)
     queries[...] = tail(hidden[...], attended, out0, up0, down0, gain(0, 1), gain(0, 2))
-    gather(low_dst, None, 6, 6, GY - 1)
+    gather(low_dst, None, 6, 6, GY)
     low = dot(order[...], low_dst[...].reshape(HALF, 256)).astype(bf16)
     summed[:, 0:HALF] = dot(swap[...], tok[...], NT) + dot(swap[...], low, NT)
     for i in range(PARTS):
@@ -328,10 +337,10 @@
         load.wait()
     half_rows = pl.ds(pl.multiple_of(plane * HALF, HALF), HALF)
     side_rows = pl.ds(pl.multiple_of((1 - plane) * HALF, HALF), HALF)
-    mine = jnp.concatenate([guess16[i] for i in range(PARTS)], axis=1)
+    held = jnp.concatenate([guess16[i] for i in range(PARTS)], axis=1)
     for c in range(4):
         at = slice(512 * c, 512 * c + 512)
-        summed[:, at] = dot(mine, coarse[half_rows, at])
+        summed[:, at] = dot(held, coarse[half_rows, at])
     for i in range(PARTS):
         remote(
             guess16.at[i], guess_dst.at[i], pair_send.at[i], pair_recv.at[i], partner
@@ -346,7 +355,7 @@
         turned[0:256, at] = (real * t_re - imag * t_im).astype(bf16)
         turned[256:512, at] = (real * t_im + imag * t_re).astype(bf16)
 
-    pl.semaphore_wait(ready, NY - 1)
+    pl.semaphore_wait(ready, GY - 1)
 
     @pl.loop(0, 4)
     def _(i):
@@ -360,20 +369,15 @@
         def _(j):
             peer = block * 16 + j
 
-            @pl.when(peer != me)
-            def _():
-                where = {"gz": peer // NY, "gy": plane * NY + lax.rem(peer, NY)}
-                remote(
-                    line_src.at[peer], line_dst.at[me], send_sem.at[3], recv_sem.at[3], where
-                ).start()
-
-    line_dst[me] = line_src[me]
+            send(
+                line_src.at[peer], line_dst.at[mine], 3, peer // NY, plane * NY + lax.rem(peer, NY)
+            )
 
     angle = cells[8:12] * (2.0 * math.pi / NZ)
     w_re, w_im = jnp.cos(angle), -jnp.sin(angle)
-    turns = lax.rem(cells[8:12].astype(jnp.int32) * me, NZ).astype(f32) * (2.0 * math.pi / NZ)
+    turns = lax.rem(cells[8:12].astype(jnp.int32) * mine, NZ).astype(f32) * (2.0 * math.pi / NZ)
     first_re, first_im = jnp.cos(turns), jnp.sin(turns)
-    gather(line_dst, None, 3, 3, GROUP - 1)
+    gather(line_dst, None, 3, 3, GROUP)
 
     def pick(i, state):
         p_re, p_im = state
@@ -398,17 +402,15 @@
         ref[z, 1] = (t_im[0] + t_im[1] + t_im[2] + t_im[3]).astype(bf16)
         return (t_re * w_re + t_im * w_im, t_im * w_re - t_re * w_im)
 
-    state = put(fix_dst, me, state)
-
     def expand(k, state):
-        z, where = in_group(k)
+        z = lax.rem(mine + k, NZ)
         state = put(fix_src, z, state)
-        remote(fix_src.at[z], fix_dst.at[me], send_sem.at[4], recv_sem.at[4], where).start()
+        send(fix_src.at[z], fix_dst.at[me], 4, 2 * (z // GY) + gy // NY, lax.rem(z, GY))
         return state
 
-    lax.fori_loop(1, GROUP, expand, state)
-
-    gather(fix_dst, None, 4, 4, GROUP - 1)
+    lax.fori_loop(0, GROUP, expand, state)
+
+    gather(fix_dst, None, 4, 4, GROUP)
     spread2[...] = fix_dst[...].reshape(GROUP * 32, 128).astype(f32)
     for c in range(4):
         at = slice(c * 256, c * 256 + 256)
@@ -448,12 +450,10 @@
             for i, block in enumerate(exchange_blocks(rows, 32)):
                 col_src[(4 * g + i) * 4 + q] = block.astype(bf16)
 
-    @pl.loop(1, GROUP)
+    @pl.loop(0, GROUP)
     def _(k):
-        peer, where = in_group(k)
-        remote(col_src.at[peer], col_dst.at[me], send_sem.at[5], recv_sem.at[5], where).start()
-
-    col_dst[me] = col_src[me]
+        peer = lax.rem(me + k, GROUP)
+        send(col_src.at[peer], col_dst.at[mine], 5, peer // NY, plane * NY + lax.rem(peer, NY))
 
     gather(relay_dst, None, 2, 2, GZ - 1)
     c_est, c_old, c_new = consts[1:2, 2:3], consts[1:2, 3:4], consts[1:2, 4:5]
@@ -469,7 +469,7 @@
         load.wait()
     patch1[...] = dot(swap[...], patch1[...]).astype(bf16)
     unpatch1[...] = dot(unpatch1[...], swap[...]).astype(bf16)
-    gather(col_dst, None, 5, 5, GROUP - 1)
+    gather(col_dst, None, 5, 5, GROUP)
     for zb in range(4):
         pix = col_dst[zb * 16 : zb * 16 + 16].reshape(256, 128)
         first = dot(pix, patch1[...], TN) + feat
@@ -506,13 +506,22 @@
         part = pl.ds(0, count)
         pltpu.make_async_copy(src.at[part], src.at[part], send_sem.at[which]).wait()
 
-    drain(high_src, 0, GY - 1)
-    drain(high_src, 1, GY - 1)
-    drain(low_src, 6, GY - 1)
+    def drain_kept(kept):
+        drain(high_src, 0, GY - kept)
+        drain(low_src, 6, GY - kept)
+        drain(line_src, 3, GROUP - kept)
+        drain(fix_src, 4, GROUP - kept)
+        drain(col_src, 5, GROUP - kept)
+
+    @pl.when(keeps)
+    def _():
+        drain_kept(1)
+
+    @pl.when(jnp.logical_not(keeps))
+    def _():
+        drain_kept(0)
+
     drain(relay_src, 2, GZ - 1)
-    drain(line_src, 3, GROUP - 1)
-    drain(fix_src, 4, GROUP - 1)
-    drain(col_src, 5, GROUP - 1)
     done = final_dst.at[:, pl.ds(0, (GY - 1) * 64), :]
     pltpu.make_async_copy(done, done, send_sem.at[7]).wait()
     pltpu.make_async_copy(done, done, recv_sem.at[7]).wait()

time: 105 us -> 88.8 us (0.85)
  Pallas kernels: 98.8 us -> 82.6 us
    pallas_call x1, Pallas kernels: 98.8 us -> 82.6 us  [local(): pl.pallas_call(step_kernel, out_shape=(shape, shape), in_specs=[vmem] * 6...]
where the time goes in v2:
time: 88.8 us; the launch traced here: 88.6 us
  Pallas kernels  82.6 us (93%)
  local copies, waits for them, and re-layouts  3.33 us (4%)
  between operations  1.97 us (2%)
    pallas_call x1, Pallas kernels, local(): pl.pallas_call(step_kernel, out_shape=(shape, shape), in_specs=[vmem] * 6...  82.6 us
    unnamed x4, local copies, waits for them, and re-layouts  3.32 us

profile of v2, /device:TPU:1, one launch (start us, length us, event | category | flops | bytes accessed | tf_op | source)
XLA Modules:
  0.0 88.6 jit_solution(8956494884301586700)
XLA Ops:
  2.0 0.1 pad_maximum_fusion.1
  2.1 0.6 pad_maximum_fusion.refs_0_
  2.7 82.6 %shard_map.212 = (f32[64,32,64]{2,1,0:T(8,128)}, f32[64,32,64]{2,1,0:T(8,128)}) custom-call(f32[2,384]{1,0:T(2,128)} %pad_maximum_fusion.refs_0_, f32[3,2,384]{2,1,0:T(2,128)} %bitcast.12, f32[256,512]{1,0:T(8,128)} %bitcast.10, f32[64,32,64]{2,1,0:T(8,128)} %bitcast.7, f32[8,32,64]{2,1,0:T(8,128)} %bitcast.11, s32[4,32,64]{2,1,0:T(8,128)} %refs_5_.1, ...), custom_call_target="tpu_custom_call" | custom-call | tf_op jit(solution)/shard_map/pallas_call | solution.py:574
  85.3 0.0 copy-start
  85.3 2.4 %copy.26 = f32[64,64,32]{1,2,0:T(8,128)} copy(f32[64,64,32]{1,2,0:T(8,128)} %bitcast.9) | data formatting | bytes 1048576
  87.6 0.0 copy-done
  87.6 1.0 %copy.27 = f32[64,64,32]{1,2,0:T(8,128)} copy(f32[64,64,32]{1,2,0:T(8,128)S(1)} %bitcast.8) | data formatting | bytes 1048576
  (3 shorter events, 0.1 us)
Async XLA Ops:
  85.3 2.4 %copy-start = (f32[64,32,64]{2,1,0:T(8,128)S(1)}, f32[64,32,64]{2,1,0:T(8,128)}, u32[]{:S(2)}) copy-start(f32[64,32,64]{2,1,0:T(8,128)} %get-tuple-element.5) | copy-start | bytes 1572868

commit v3 on v2

--- a/solution.py
+++ b/solution.py
@@ -167,14 +167,14 @@
 
 def step_kernel(*refs):
     (
-        consts, gains, noisy, noise, measured, cap,
+        consts, gains, noisy, measured, cap, h_noise,
         h_patch, h_qkv, h_out, h_up, h_down, h_unpatch,
         h_coarse, h_twist, h_fine, h_fine_t, h_order, h_swap, h_cast, h_deal, h_spill,
-        previous, estimate,
+        base, scaled,
         patch0, qkv0, out0, up0, down0, unpatch0,
         patch1, qkv1, out1, up1, down1, unpatch1,
         coarse, twist, fine, fine_t, order, swap, cast, deal, spill,
-        strips, wide, cut, high_src, low_src, own_dst, oth_dst, low_dst, relay_src, relay_dst,
+        noise, strips, wide, cut, high_src, low_src, own_dst, oth_dst, low_dst, relay_src, relay_dst,
         tok, hidden, queries, pairs, guess, guess16, guess_dst,
         summed, turned, spread, line_src, line_dst,
         cells, fix_src, fix_dst, turned2, spread2, back_src, back_dst, blended,
@@ -197,7 +197,7 @@
         (h_fine.at[plane], fine), (h_fine_t.at[plane], fine_t),
         (h_patch.at[1], patch1), (h_qkv.at[1], qkv1), (h_out.at[1], out1), (h_up.at[1], up1),
         (h_down.at[1], down1), (h_unpatch.at[1], unpatch1), (h_deal, deal),
-        (h_spill, spill),
+        (h_spill, spill), (h_noise, noise),
     ]
     loads = [
         pltpu.make_async_copy(src, dst, load_sem.at[i]) for i, (src, dst) in enumerate(plan)
@@ -455,18 +455,21 @@
         peer = lax.rem(me + k, GROUP)
         send(col_src.at[peer], col_dst.at[mine], 5, peer // NY, plane * NY + lax.rem(peer, NY))
 
+    for load in loads[13:]:
+        load.wait()
     gather(relay_dst, None, 2, 2, GZ - 1)
-    c_est, c_old, c_new = consts[1:2, 2:3], consts[1:2, 3:4], consts[1:2, 4:5]
+    c_old, c_new, inv_noise = consts[1:2, 3:4], consts[1:2, 4:5], consts[1:2, 5:6]
 
     @pl.loop(0, GZ)
     def _(i):
         for z in range(4):
-            previous[4 * i + z] = (
+            noise[4 * i + z] = (
                 c_old * relay_dst[i, :, 64 * z : 64 * z + 64] + c_new * noise[4 * i + z]
             )
 
-    for load in loads[13:]:
-        load.wait()
+    store = pltpu.make_async_copy(noise, base, load_sem.at[len(plan)])
+    store.start()
+
     patch1[...] = dot(swap[...], patch1[...]).astype(bf16)
     unpatch1[...] = dot(unpatch1[...], swap[...]).astype(bf16)
     gather(col_dst, None, 5, 5, GROUP)
@@ -488,10 +491,11 @@
         attended = jnp.concatenate(attended, axis=0)
         normed = tail(hidden[half, :], attended, out1, up1, down1, gain(1, 1), gain(1, 2))
         moved = dot(deal[...], normed).astype(bf16)
-        value = root_noise * dot(moved, unpatch1[...])
+        value = jnp.zeros((256, 256), f32)
         for zb in range(4):
             pix = col_dst[zb * 16 : zb * 16 + 16].reshape(256, 128)
             value = value + dot(spill[p, :, 128 * zb : 128 * zb + 128], pix, NT)
+        value = value * inv_noise + dot(moved, unpatch1[...])
         for h in range(2):
             final_src[p, :, h] = value[:, 128 * h : 128 * h + 128].reshape(GY, 32, 128)
         here = pl.ds(pl.multiple_of(gy * 64 + p * 32, 32), 32)
@@ -537,8 +541,8 @@
                     for part in range(2):
                         z = zb * 16 + h * 8 + part * 4 + i
                         value = block[:, 64 * part : 64 * part + 64]
-                        estimate[z, at, :] = value
-                        previous[z, at, :] = previous[z, at, :] + c_est * value
+                        scaled[z, at, :] = value
+    store.wait()
 
 
 def local(
@@ -556,7 +560,7 @@
     spread = jnp.sqrt((1.0 - signal_prev) / (1.0 - signal_now) * (1.0 - signal_now / signal_prev))
     coefs = (
         root_noise, 1.0 / root_signal, jnp.sqrt(signal_prev) - toward * root_signal / root_noise,
-        toward / root_noise, spread,
+        toward / root_noise, spread, 1.0 / root_noise,
     )
     place = lax.broadcasted_iota(jnp.int32, (1, D), 1)
     row = jnp.zeros((1, D), f32)
@@ -571,15 +575,16 @@
         V((FF, D), bf16), V((D, PIX), bf16),
     ]
     shape = jax.ShapeDtypeStruct((NZ, 32, 64), f32)
-    previous, estimate = pl.pallas_call(
+    base, scaled = pl.pallas_call(
         step_kernel,
         out_shape=(shape, shape),
-        in_specs=[vmem] * 6 + [anywhere] * 15,
-        out_specs=(vmem, vmem),
+        in_specs=[vmem] * 5 + [anywhere] * 16,
+        out_specs=(anywhere, vmem),
         scratch_shapes=weights() + weights() + [
             V((1024, 2048), bf16), V((2, 256, 1024), f32), V((256, 512), bf16),
             V((512, 256), bf16), V((512, 512), bf16), V((256, 256), bf16),
             V((512, 512), bf16), V((256, 256), bf16), V((2, 256, 512), bf16),
+            V((NZ, 32, 64), f32),
             V((4, 256, 128), f32), V((12, 32, 128), f32), V((512, 512), bf16),
             V((GY, 64, 256), bf16), V((GY, 64, 256), bf16), V((GY, 64, 256), bf16),
             V((GY, 64, 256), bf16), V((GY, 64, 256), bf16),
@@ -594,7 +599,7 @@
             V((2, PIX, 256), bf16), V((PIX, HALF), f32),
             V((GROUP, 16, 128), bf16), V((GROUP, 16, 128), bf16),
             V((2, GY, 2, 32, 128), f32), V((2, 512, 128), f32),
-            pltpu.SemaphoreType.DMA((21,)), pltpu.SemaphoreType.DMA((8,)),
+            pltpu.SemaphoreType.DMA((23,)), pltpu.SemaphoreType.DMA((8,)),
             pltpu.SemaphoreType.DMA((8,)), pltpu.SemaphoreType.DMA((PARTS + 2,)),
             pltpu.SemaphoreType.DMA((PARTS + 2,)), pltpu.SemaphoreType.REGULAR,
         ],
@@ -602,10 +607,12 @@
             collective_id=0, has_side_effects=True, vmem_limit_bytes=58 * MIB
         ),
     )(
-        consts, norm_gain.transpose(1, 0, 2), noisy.reshape(256, LAT), noise.transpose(0, 2, 1),
-        measured.reshape(8, 32, 64), cap_index,
+        consts, norm_gain.transpose(1, 0, 2), noisy.reshape(256, LAT),
+        measured.reshape(8, 32, 64), cap_index, noise.transpose(0, 2, 1),
         w_patch, w_qkv, w_out, w_up, w_down, w_unpatch, *(jnp.asarray(t) for t in tables()),
     )
+    estimate = root_noise * scaled
+    previous = base + (coefs[2] * root_noise) * scaled
     return (previous.transpose(0, 2, 1), estimate.transpose(0, 2, 1))
 
 

time: 88.8 us -> 87.5 us (0.985)
  local copies, waits for them, and re-layouts: 3.33 us -> 0.01 us
  other arithmetic: 0.72 us -> 3.83 us
  Pallas kernels: 82.6 us -> 81.5 us
    unnamed x4 -> x0, local copies, waits for them, and re-layouts: 3.32 us -> none
    transpose x0 -> x1, other arithmetic: none -> 3.11 us  [local(): return (previous.transpose(0, 2, 1), estimate.transpose(0, 2, 1))]
    pallas_call x1, Pallas kernels: 82.6 us -> 81.5 us  [local(): pl.pallas_call(step_kernel, out_shape=(shape, shape), in_specs=[vmem] * 5...]
where the time goes in v3:
time: 87.5 us; the launch traced here: 87.4 us
  Pallas kernels  81.5 us (93%)
  other arithmetic  3.83 us (4%)
  between operations  2 us (2%)
    pallas_call x1, Pallas kernels, local(): pl.pallas_call(step_kernel, out_shape=(shape, shape), in_specs=[vmem] * 5...  81.5 us
    transpose x1, other arithmetic, local(): return (previous.transpose(0, 2, 1), estimate.transpose(0, 2, 1))  3.11 us

profile of v3, /device:TPU:1, one launch (start us, length us, event | category | flops | bytes accessed | tf_op | source)
XLA Modules:
  0.0 87.4 jit_solution(10687249747601458026)
XLA Ops:
  2.0 0.1 pad_maximum_fusion.1
  2.1 0.6 pad_maximum_fusion.refs_0_
  2.7 81.5 %shard_map.212 = (f32[64,32,64]{2,1,0:T(8,128)}, f32[64,32,64]{2,1,0:T(8,128)}) custom-call(f32[2,384]{1,0:T(2,128)} %pad_maximum_fusion.refs_0_, f32[3,2,384]{2,1,0:T(2,128)} %bitcast.12, f32[256,512]{1,0:T(8,128)} %bitcast.10, f32[8,32,64]{2,1,0:T(8,128)} %bitcast.11, s32[4,32,64]{2,1,0:T(8,128)} %refs_4_.1, f32[64,32,64]{2,1,0:T(8,128)} %bitcast.9, ...), custom_call_target="tpu_custom_call" | custom-call | tf_op jit(solution)/shard_map/pallas_call | solution.py:578
  84.3 3.1 %multiply_bitcast_fusion = (f32[64,64,32]{1,2,0:T(8,128)}, f32[64,64,32]{1,2,0:T(8,128)}) fusion(f32[64,32,64]{2,1,0:T(8,128)} %get-tuple-element.5, f32[]{:T(128)S(6)} %sqrt.15, f32[64,32,64]{2,1,0:T(8,128)} %get-tuple-element.4, f32[]{:T(128)S(6)} %mul.49), kind=kLoop, calls=%fused_computation | loop fusion | flops 393216 | bytes 2097160 | tf_op jit(solution)/shard_map/transpose | solution.py:616
  (3 shorter events, 0.1 us)

commit v4 on v3

--- a/solution.py
+++ b/solution.py
@@ -320,9 +320,7 @@
     left = lax.broadcasted_iota(jnp.int32, (HALF, 128), 1) < 64
     attended = attention(queries[...], pairs[:, :D], pairs[:, D:], left)
     queries[...] = tail(hidden[...], attended, out0, up0, down0, gain(0, 1), gain(0, 2))
-    gather(low_dst, None, 6, 6, GY)
-    low = dot(order[...], low_dst[...].reshape(HALF, 256)).astype(bf16)
-    summed[:, 0:HALF] = dot(swap[...], tok[...], NT) + dot(swap[...], low, NT)
+    summed[:, 0:HALF] = dot(swap[...], tok[...], NT)
     for i in range(PARTS):
         at = slice(i * CHUNK, i * CHUNK + CHUNK)
         net = dot(unpatch0[...], queries[at, :], (((0,), (1,)), ((), ())))
@@ -377,6 +375,9 @@
     w_re, w_im = jnp.cos(angle), -jnp.sin(angle)
     turns = lax.rem(cells[8:12].astype(jnp.int32) * mine, NZ).astype(f32) * (2.0 * math.pi / NZ)
     first_re, first_im = jnp.cos(turns), jnp.sin(turns)
+    gather(low_dst, None, 6, 6, GY)
+    low = dot(order[...], low_dst[...].reshape(HALF, 256)).astype(bf16)
+    guess[...] = guess[...] + dot(swap[...], low, NT) * inv_signal
     gather(line_dst, None, 3, 3, GROUP)
 
     def pick(i, state):

time: 87.5 us -> 87.2 us (level)
  no operation moved by 1% of the time
where the time goes in v4:
time: 87.2 us; the launch traced here: 87 us
  Pallas kernels  81.1 us (93%)
  other arithmetic  3.83 us (4%)
  between operations  2 us (2%)
    pallas_call x1, Pallas kernels, local(): pl.pallas_call(step_kernel, out_shape=(shape, shape), in_specs=[vmem] * 5...  81.1 us
    transpose x1, other arithmetic, local(): return (previous.transpose(0, 2, 1), estimate.transpose(0, 2, 1))  3.11 us

profile of v4, /device:TPU:1, one launch (start us, length us, event | category | flops | bytes accessed | tf_op | source)
XLA Modules:
  0.0 87.0 jit_solution(6996447273530852509)
XLA Ops:
  2.0 0.1 pad_maximum_fusion.1
  2.1 0.6 pad_maximum_fusion.refs_0_
  2.7 81.1 %shard_map.212 = (f32[64,32,64]{2,1,0:T(8,128)}, f32[64,32,64]{2,1,0:T(8,128)}) custom-call(f32[2,384]{1,0:T(2,128)} %pad_maximum_fusion.refs_0_, f32[3,2,384]{2,1,0:T(2,128)} %bitcast.12, f32[256,512]{1,0:T(8,128)} %bitcast.10, f32[8,32,64]{2,1,0:T(8,128)} %bitcast.11, s32[4,32,64]{2,1,0:T(8,128)} %refs_4_.1, f32[64,32,64]{2,1,0:T(8,128)} %bitcast.9, ...), custom_call_target="tpu_custom_call" | custom-call | tf_op jit(solution)/shard_map/pallas_call | solution.py:579
  83.9 3.1 %multiply_bitcast_fusion = (f32[64,64,32]{1,2,0:T(8,128)}, f32[64,64,32]{1,2,0:T(8,128)}) fusion(f32[64,32,64]{2,1,0:T(8,128)} %get-tuple-element.5, f32[]{:T(128)S(6)} %sqrt.15, f32[64,32,64]{2,1,0:T(8,128)} %get-tuple-element.4, f32[]{:T(128)S(6)} %mul.49), kind=kLoop, calls=%fused_computation | loop fusion | flops 393216 | bytes 2097160 | tf_op jit(solution)/shard_map/transpose | solution.py:617
  (3 shorter events, 0.1 us)
